TPU v7x, 32 devices: a whole 2x2x4 slice. The times are simulated.
32 devices in a mesh: gx: 2 (over y), gy: 4 (over z), pa: 4 (over x, core).
Axes of the slice: x: 2, y: 2, z: 4, core: 2. Of those that a mesh axis runs over, the one named last changes fastest.
Arguments:
- latents: bfloat16 [32, 128, 768], P(('gx', 'pa'), 'gy'), may hold values from -6 to 6
- noise: bfloat16 [2, 32, 128, 768], P(None, ('gx', 'pa'), 'gy'), may hold values from -6 to 6
- proc_gain: float32 [768], replicated, may hold values from 0.1 to 1.9
- w_qkv: bfloat16 [768, 2304], P(('gx', 'pa')), may hold values from -0.21875 to 0.21875
- w_out: bfloat16 [768, 768], P(('gx', 'pa')), may hold values from -0.21875 to 0.21875
- w_query: bfloat16 [128, 768], P(('gx', 'pa')), may hold values from -0.5 to 0.5
- w_head: bfloat16 [768, 3], P(('gx', 'pa')), may hold values from -0.21875 to 0.21875
- probe_cell: int32 [32768], P(('gx', 'gy', 'pa')), may hold values from 0 to 127
- probe_offset: float32 [2, 32768], P(None, ('gx', 'gy', 'pa')), may hold values from 0 to 1
- probe_count: int32 [32], P(('gx', 'gy', 'pa')), may hold values from 128 to 1024, as said below
Outputs:
- latent_out: bfloat16 [32, 128, 768], P(('gx', 'pa'), 'gy')
- probe_values: float32 [3, 32768], P(None, ('gx', 'gy', 'pa'))
Inputs may be any that keep to these rules, and one draw needn't show every extreme that they name: `probe_cell`: a cell of the device's own 4 x 32 block, numbered row by row. `probe_count`: slots below the count hold probes, the others are empty; in every draw one device has all 1024 slots live.
All inputs are finite; a program needn't handle non-finite values.
Results may differ from a plain program's by a relative error of at most 0.02.
Values may be sent and summed in bfloat16 or wider, within the bound.
A program may use at most 64 MiB of HBM per device.

v0:
```python
import functools
import math

import jax
import jax.numpy as jnp
import numpy as np
from jax import lax
from jax.experimental import pallas as pl
from jax.experimental.pallas import tpu as pltpu
from jax.sharding import PartitionSpec as P

HEADS = 12
FQ = 128
CH = 3
RAD = 3
STEPS = 2
EPS = 1e-06
NOISE_COEF = 0.3
MESH = pl.DeviceIdType.MESH
FAR = -1e30
LANES = 128
SIDES = [(dr, dc) for dc in (-1, 1) for dr in (-1, 0, 1)]
F32 = jnp.float32
BF16 = jnp.bfloat16


def side_rows(rows, width):
    return -(-(rows + 2 * width) * width // 8) * 8


def side_cells(rows, cols, width):
    held = side_rows(rows, width)
    places = []
    for first in (-width, cols):
        group = [(r, first + c) for r in range(-width, rows + width) for c in range(width)]
        places += group + [None] * (held - len(group))
    return places


def halo_cells(rows, cols, width):
    own = [(r, c) for r in range(rows) for c in range(cols)]
    above = [(r, c) for r in range(-width, 0) for c in range(cols)]
    below = [(r, c) for r in range(rows, rows + width) for c in range(cols)]
    return own + above + below + side_cells(rows, cols, width)


def packet_table(rows, cols, width):
    places = side_cells(rows, cols, width)
    table = np.zeros((len(SIDES), len(places), rows * cols), np.float32)
    for number, (dr, dc) in enumerate(SIDES):
        for place, cell in enumerate(places):
            if cell is None:
                continue
            r, c = cell[0] + dr * rows, cell[1] + dc * cols
            if 0 <= r < rows and 0 <= c < cols:
                table[number, place, r * cols + c] = 1.0
    return table


def window_bias(rows, cols, width):
    cells = halo_cells(rows, cols, width)
    bias = np.full((len(cells), rows * cols), FAR, np.float32)
    for place, cell in enumerate(cells):
        if cell is None:
            continue
        for r in range(rows):
            for c in range(cols):
                if abs(cell[0] - r) <= width and abs(cell[1] - c) <= width:
                    bias[place, r * cols + c] = 0.0
    return bias


def sine_terms(t):
    z = (t * t) * (4.0 * math.pi * math.pi)
    odd = jnp.full_like(t, -1.0 / math.factorial(15))
    for power in range(13, 0, -2):
        odd = odd * z + (-1.0) ** (power // 2) / math.factorial(power)
    even = jnp.full_like(t, 1.0 / math.factorial(16))
    for power in range(14, -1, -2):
        even = even * z + (-1.0) ** (power // 2) / math.factorial(power)
    return odd * (t * (2.0 * math.pi)), even


def dot(a, b):
    return lax.dot_general(a, b, (((1,), (0,)), ((), ())), preferred_element_type=F32)


def dot_t(a, b):
    return lax.dot_general(a, b, (((1,), (1,)), ((), ())), preferred_element_type=F32)


def body(dims, gather, *refs):
    n_gx, n_gy, n_pa, rows, cols, model = dims
    (lat_ref, noise_ref, gain_ref, cell_ref, offset_ref, near_bias_ref, probe_bias_ref, near_pick_ref,
     probe_pick_ref, *refs) = refs
    weight_in, refs = refs[:4], refs[4:]
    out_ref, val_ref, *refs = refs
    if gather:
        weights, refs = refs[:4], refs[4:]
        w_send, w_recv, *refs = refs
    else:
        weights = weight_in
    (held0, held1, held2, got0, got1, got2, pack0, pack1, pack2, h_send, h_recv, normed, q_s, kv_s, att_s,
     hot_s, feat_s, qt_s, ut_s) = refs
    held, got, pack = (held0, held1, held2), (got0, got1, got2), (pack0, pack1, pack2)
    own = rows * cols
    gx, gy, pa = lax.axis_index("gx"), lax.axis_index("gy"), lax.axis_index("pa")
    ring = n_gx * n_pa
    place = gx * n_pa + pa

    def device(dr, dc):
        r = lax.rem(place + dr + ring, ring)
        return (lax.div(r, n_pa), lax.rem(gy + dc + n_gy, n_gy), lax.rem(r, n_pa))

    around = [device(-1, 0), device(1, 0)] + [device(dr, dc) for dr, dc in SIDES]
    partners = list(around)
    if gather:
        pa_x = lax.rem(pa + 2, 4)
        to_x, to_y = (gx, gy, pa_x), (1 - gx, gy, pa)
        to_twin = (gx, gy, pa + 1 - 2 * lax.rem(pa, 2))
        partners += [to_x, to_y, to_twin]
    barrier = pltpu.get_barrier_semaphore()
    for target in partners:
        pl.semaphore_signal(barrier, inc=1, device_id=target, device_id_type=MESH)
    pl.semaphore_wait(barrier, len(partners))

    started = []

    def push(src, dst, send, recv, target):
        copy = pltpu.make_async_remote_copy(
            src_ref=src, dst_ref=dst, send_sem=send, recv_sem=recv, device_id=target, device_id_type=MESH
        )
        copy.start()
        started.append(copy)
        return copy

    def widths(number):
        return RAD if number < STEPS else 1

    def halo_start(number, source):
        width = widths(number)
        span = width * cols
        here, sems = held[number], (h_send.at[number], h_recv.at[number])
        copies = [
            push(source.at[pl.ds(0, span)], here.at[pl.ds(own + span, span)], sems[0].at[0], sems[1].at[0], around[0]),
            push(source.at[pl.ds(own - span, span)], here.at[pl.ds(own, span)], sems[0].at[1], sems[1].at[1], around[1]),
        ]
        pick = (near_pick_ref if number < STEPS else probe_pick_ref)
        tail = pack[number].shape[1]
        value = source[...]
        for k in range(len(SIDES)):
            pack[number][k] = dot(pick[k], value).astype(BF16)
        for k in range(len(SIDES)):
            copies.append(
                push(pack[number].at[k], got[number].at[k], sems[0].at[2 + k], sems[1].at[2 + k], around[2 + k])
            )
        return copies

    def halo_end(number, copies):
        for copy in copies:
            copy.wait_recv()
        total = got[number][0].astype(F32)
        for k in range(1, len(SIDES)):
            total = total + got[number][k].astype(F32)
        tail = total.shape[0]
        base = own + 2 * widths(number) * cols
        held[number][pl.ds(base, tail)] = total.astype(BF16)

    class Moves:
        def __init__(self, number):
            self.number, self.ref = number, weights[number]
            half = self.ref.shape[1] // 2
            self.cut = half if half % 16 == 0 else None
            self.slot = {}

        def go(self, slot, part, target, lo=None, size=None):
            view = self.ref.at[part] if lo is None else self.ref.at[part, pl.ds(lo, size)]
            self.slot[slot] = push(view, view, w_send.at[self.number, slot], w_recv.at[self.number, slot], target)

        def begin(self):
            self.go(0, place, to_x)
            self.go(1, place, to_y)
            self.go(2, place, to_twin)

        def middle(self):
            near_x, near_y = gx * 4 + pa_x, (1 - gx) * 4 + pa
            self.slot[0].wait_recv()
            if self.cut is None:
                self.go(3, near_x, to_y)
            else:
                self.go(3, near_x, to_y, 0, self.cut)
            self.go(5, near_x, to_twin)
            self.slot[1].wait_recv()
            if self.cut is not None:
                self.go(4, near_y, to_x, self.cut, self.cut)
            self.go(6, near_y, to_twin)

        def end(self):
            across = (1 - gx) * 4 + pa_x
            self.slot[3].wait_recv()
            if self.cut is None:
                self.go(7, across, to_twin)
            else:
                self.go(7, across, to_twin, 0, self.cut)
                self.slot[4].wait_recv()
                self.go(8, across, to_twin, self.cut, self.cut)

        def finish(self):
            for slot in (2, 5, 6, 7, 8):
                if slot in self.slot:
                    self.slot[slot].wait_recv()

    if gather:
        moves = [Moves(number) for number in range(4)]
        weights[0][place] = weight_in[0][...]
        moves[0].begin()
        for number in (1, 2):
            weights[number][place] = weight_in[number][...]
        weights[3][place] = jnp.zeros(weights[3].shape[1:], BF16)
        weights[3][place, :, 0:CH] = weight_in[3][...]

    halo = halo_start(0, lat_ref)
    held[0][pl.ds(0, own)] = lat_ref[...]

    slots = cell_ref.shape[1]
    cells = lax.broadcasted_iota(jnp.int32, (own, slots), 0)
    hot_s[...] = jnp.where(cells == cell_ref[...], 1.0, 0.0).astype(BF16)
    quarter = FQ // 4
    freq = lax.broadcasted_iota(jnp.int32, (quarter, slots), 0).astype(F32) + 1.0
    for axis in range(2):
        turns = freq * offset_ref[pl.ds(axis, 1), :]
        sine, cosine = sine_terms(turns - jnp.floor(turns + 0.5))
        feat_s[pl.ds(2 * axis * quarter, quarter)] = sine.astype(BF16)
        feat_s[pl.ds((2 * axis + 1) * quarter, quarter)] = cosine.astype(BF16)

    def normalize(number):
        values = held[number][...].astype(F32)
        factor = lax.rsqrt(jnp.mean(values * values, axis=-1, keepdims=True) + EPS)
        normed[...] = (values * factor * gain_ref[...]).astype(BF16)

    def whole(number):
        ref = weights[number]
        return ref[...].reshape(-1, ref.shape[-1])

    def columns(number, start, size):
        ref = weights[number]
        if len(ref.shape) == 3:
            return ref[:, :, pl.ds(start, size)].reshape(model, size)
        return ref[:, pl.ds(start, size)]

    pairs = model // LANES
    keys = kv_s.shape[0]
    tile = 256
    scale = 1.0 / math.sqrt(model // HEADS)

    def project():
        def queries(i, carry):
            start = pl.multiple_of(i * tile, tile)
            q_s[:, pl.ds(start, tile)] = (dot(normed[pl.ds(0, own)], columns(0, start, tile)) * scale).astype(BF16)
            return carry

        def key_values(i, carry):
            start = pl.multiple_of(i * tile, tile)
            kv_s[:, pl.ds(start, tile)] = dot(normed[...], columns(0, model + start, tile)).astype(BF16)
            return carry

        lax.fori_loop(0, model // tile, queries, 0)
        lax.fori_loop(0, 2 * model // tile, key_values, 0)

    def attend():
        lane = lax.broadcasted_iota(jnp.int32, (own, LANES), 1)
        low = lane < LANES // 2
        unit = jnp.where(lane == lax.broadcasted_iota(jnp.int32, (own, LANES), 0), 1.0, 0.0).astype(BF16)
        zero = jnp.zeros((own, LANES), BF16)
        ones = jnp.ones((keys, LANES), BF16)

        def pair(i, carry):
            start = pl.multiple_of(i * LANES, LANES)
            query = q_s[:, pl.ds(start, LANES)]
            both = jnp.concatenate(
                [
                    jnp.concatenate([unit, jnp.where(low, query, zero)], axis=1),
                    jnp.concatenate([unit, jnp.where(low, zero, query)], axis=1),
                ],
                axis=0,
            )
            key = jnp.concatenate([near_bias_ref[...], kv_s[:, pl.ds(start, LANES)]], axis=1)
            scores = dot_t(both, key)
            top = jnp.max(scores, axis=1, keepdims=True)
            weight = jnp.exp(scores - top).astype(BF16)
            value = jnp.concatenate(
                [kv_s[:, pl.ds(pl.multiple_of(model + start, LANES), LANES)], ones], axis=1
            )
            mixed = dot(weight, value)
            mixed = mixed[:, :LANES] / mixed[:, LANES:]
            att_s[:, pl.ds(start, LANES)] = jnp.where(low, mixed[:own], mixed[own:]).astype(BF16)
            return carry

        lax.fori_loop(0, pairs, pair, 0, unroll=2)

    def update(step, target):
        for start in range(0, model, tile):
            cut = pl.ds(start, tile)
            moved = dot(att_s[...], columns(1, start, tile))
            target[pl.ds(0, own), cut] = (
                held[step][pl.ds(0, own), cut].astype(F32)
                + moved / STEPS
                + NOISE_COEF * noise_ref[step, :, cut].astype(F32)
            ).astype(BF16)

    if gather:
        moves[0].middle()
        for number in (1, 2, 3):
            moves[number].begin()
    halo_end(0, halo)
    normalize(0)
    if gather:
        moves[0].end()
        moves[0].finish()
    project()
    if gather:
        for number in (1, 2, 3):
            moves[number].middle()
    attend()
    if gather:
        for number in (1, 2, 3):
            moves[number].end()
        moves[1].finish()
    update(0, held[1])
    halo = halo_start(1, held[1].at[pl.ds(0, own)])
    if gather:
        moves[2].finish()
        moves[3].finish()
    turned = whole(2).astype(F32).T.astype(BF16)
    for start in range(0, slots, tile):
        qt_s[:, pl.ds(start, tile)] = (dot(turned, feat_s[:, pl.ds(start, tile)]) * scale).astype(BF16)
    halo_end(1, halo)
    normalize(1)
    project()
    attend()
    update(1, held[2])
    halo = halo_start(2, held[2].at[pl.ds(0, own)])
    out_ref[...] = held[2][pl.ds(0, own)]
    halo_end(2, halo)

    near = held[2].shape[0]
    head = weights[3]
    half = LANES // 2
    for i in range(pairs):
        context = held[2][:, pl.ds(i * LANES, LANES)]
        matrix = whole(3)[i * LANES : (i + 1) * LANES]
        row = lax.broadcasted_iota(jnp.int32, matrix.shape, 0)
        for side in range(2):
            kept = jnp.where((row < half) == (side == 0), matrix, jnp.zeros_like(matrix))
            turned = dot(context, kept).T[0:16]
            line = lax.broadcasted_iota(jnp.int32, turned.shape, 0)
            ut_s[2 * i + side] = jnp.where(line == CH, 1.0, turned).astype(BF16)

    val_ref[...] = jnp.zeros_like(val_ref)

    def decode(i, carry):
        start = pl.multiple_of(i * LANES, LANES)
        key = jnp.concatenate([probe_bias_ref[...], held[2][:, pl.ds(start, LANES)]], axis=1)
        for first in range(0, slots, tile):
            cut = pl.ds(first, tile)
            hot = hot_s[:, cut]
            blank = jnp.zeros((half, tile), BF16)
            total = val_ref[:, cut]
            for side in range(2):
                query = qt_s[pl.ds(pl.multiple_of(start + side * half, half), half), cut]
                parts = [hot, query, blank] if side == 0 else [hot, blank, query]
                scores = dot(key, jnp.concatenate(parts, axis=0))
                top = jnp.max(scores, axis=0, keepdims=True)
                weight = jnp.exp(scores - top).astype(BF16)
                mixed = dot(ut_s[2 * i + side], weight)
                total = total + mixed[0:8] / mixed[CH : CH + 1]
            val_ref[:, cut] = total
        return carry

    lax.fori_loop(0, pairs, decode, 0)
    for copy in started:
        copy.wait_send()


def local(sizes, latents, noise, proc_gain, w_qkv, w_out, w_query, w_head, probe_cell, probe_offset, probe_count):
    n_gx, n_gy, n_pa = sizes
    rows, cols, model = latents.shape
    own = rows * cols
    slots = probe_cell.shape[0]
    shards = [w_qkv, w_out, w_query, w_head]
    gather = n_gx == 2 and n_pa == 4 and all(shard.shape[0] % 16 == 0 for shard in shards)
    count = n_gx * n_pa
    if not gather:
        shards = [lax.all_gather(shard, ("gx", "pa"), axis=0, tiled=True) for shard in shards]
        shards[3] = jnp.pad(shards[3], ((0, 0), (0, LANES - CH)))
    near = len(halo_cells(rows, cols, RAD))
    close = len(halo_cells(rows, cols, 1))
    side_near, side_close = 2 * side_rows(rows, RAD), 2 * side_rows(rows, 1)
    tables = [
        jnp.asarray(table, BF16)
        for table in (
            window_bias(rows, cols, RAD),
            window_bias(rows, cols, 1),
            packet_table(rows, cols, RAD),
            packet_table(rows, cols, 1),
        )
    ]
    scratch = []
    if gather:
        scratch += [pltpu.VMEM((count,) + shard.shape, BF16) for shard in shards[:3]]
        scratch += [pltpu.VMEM((count, w_head.shape[0], LANES), BF16)]
        scratch += [pltpu.SemaphoreType.DMA((4, 9)), pltpu.SemaphoreType.DMA((4, 9))]
    scratch += [pltpu.VMEM((size, model), BF16) for size in (near, near, close)]
    for _ in range(2):
        scratch += [pltpu.VMEM((len(SIDES), size, model), BF16) for size in (side_near, side_near, side_close)]
    scratch += [pltpu.SemaphoreType.DMA((STEPS + 1, 8)), pltpu.SemaphoreType.DMA((STEPS + 1, 8))]
    scratch += [
        pltpu.VMEM((near, model), BF16),
        pltpu.VMEM((own, model), BF16),
        pltpu.VMEM((near, 2 * model), BF16),
        pltpu.VMEM((own, model), BF16),
        pltpu.VMEM((own, slots), BF16),
        pltpu.VMEM((FQ, slots), BF16),
        pltpu.VMEM((model, slots), BF16),
        pltpu.VMEM((HEADS, 16, close), BF16),
    ]
    operands = [
        latents.reshape(own, model),
        noise.reshape(STEPS, own, model),
        proc_gain.reshape(1, model),
        probe_cell.reshape(1, slots),
        probe_offset,
        *tables,
        *shards,
    ]
    latent_out, values = pl.pallas_call(
        functools.partial(body, (n_gx, n_gy, n_pa, rows, cols, model), gather),
        out_shape=(jax.ShapeDtypeStruct((own, model), BF16), jax.ShapeDtypeStruct((8, slots), F32)),
        in_specs=[pl.BlockSpec(memory_space=pltpu.VMEM)] * len(operands),
        out_specs=[pl.BlockSpec(memory_space=pltpu.VMEM)] * 2,
        scratch_shapes=scratch,
        compiler_params=pltpu.CompilerParams(
            collective_id=0, has_side_effects=True, vmem_limit_bytes=48 * 1024 * 1024
        ),
        cost_estimate=pl.CostEstimate(flops=6_000_000_000, bytes_accessed=4_000_000, transcendentals=4_000_000),
    )(*operands)
    live = jnp.arange(slots, dtype=jnp.int32) < probe_count[0]
    probe_values = jnp.where(live[None, :], values[:CH], jnp.zeros((), F32))
    return (latent_out.reshape(rows, cols, model), probe_values)


def solution(mesh):
    sizes = (mesh.shape["gx"], mesh.shape["gy"], mesh.shape["pa"])
    return jax.shard_map(
        functools.partial(local, sizes),
        mesh=mesh,
        in_specs=(
            P(("gx", "pa"), "gy", None),
            P(None, ("gx", "pa"), "gy", None),
            P(),
            P(("gx", "pa"), None),
            P(("gx", "pa"), None),
            P(("gx", "pa"), None),
            P(("gx", "pa"), None),
            P(("gx", "gy", "pa")),
            P(None, ("gx", "gy", "pa")),
            P(("gx", "gy", "pa")),
        ),
        out_specs=(P(("gx", "pa"), "gy", None), P(None, ("gx", "gy", "pa"))),
        check_vma=False,
    )
```

profile of v0, /device:TPU:0, one launch (start us, length us, event | category | flops | bytes accessed | tf_op | source)
XLA Modules:
  0.0 90.3 jit_solution(271546380867397200)
XLA Ops:
  0.6 0.0 copy-start.4
  0.6 0.8 copy.16.refs_12_
  1.4 0.0 copy-start.5
  1.4 0.7 reshape.25.refs_2_
  2.1 0.0 copy-start.6
  2.2 0.0 copy-done.4
  2.2 0.0 copy-done.5
  2.2 0.7 copy-done.6
  2.8 0.0 copy-start
  2.8 1.0 %copy-done = bf16[96,2304]{1,0:T(8,128)(2,1)S(1)} copy-done((bf16[96,2304]{1,0:T(8,128)(2,1)S(1)}, bf16[96,2304]{1,0:T(8,128)(2,1)}, u32[]{:S(2)}) %copy-start) | copy-done | bytes 442392
  3.9 0.0 copy-start.1
  3.9 1.0 %copy-done.1 = bf16[2,4,32,768]{3,2,1,0:T(8,128)(2,1)S(1)} copy-done((bf16[2,4,32,768]{3,2,1,0:T(8,128)(2,1)S(1)}, bf16[2,4,32,768]{3,2,1,0:T(8,128)(2,1)}, u32[]{:S(2)}) %copy-start.1) | copy-done | bytes 393240
  4.8 0.0 copy-start.2
  4.8 0.9 %copy-done.2 = bf16[4,32,768]{2,1,0:T(8,128)(2,1)S(1)} copy-done((bf16[4,32,768]{2,1,0:T(8,128)(2,1)S(1)}, bf16[4,32,768]{2,1,0:T(8,128)(2,1)}, u32[]{:S(2)}) %copy-start.2) | copy-done | bytes 196632
  5.8 0.0 copy-start.3
  5.8 0.9 %copy-done.3 = bf16[96,768]{1,0:T(8,128)(2,1)S(1)} copy-done((bf16[96,768]{1,0:T(8,128)(2,1)S(1)}, bf16[96,768]{1,0:T(8,128)(2,1)}, u32[]{:S(2)}) %copy-start.3) | copy-done | bytes 147480
  6.7 0.0 copy-start.7
  6.7 0.9 copy-done.7
  7.6 0.0 copy-start.8
  7.6 0.9 copy-done.8
  8.5 0.0 copy-start.9
  8.5 0.8 copy-done.9
  9.3 0.0 copy-start.10
  9.3 0.7 copy-done.10
  10.0 78.4 %shard_map.149 = (bf16[128,768]{1,0:T(8,128)(2,1)S(1)}, f32[8,1024]{1,0:T(8,128)S(1)}) custom-call(bf16[128,768]{1,0:T(8,128)(2,1)S(1)} %bitcast.8, bf16[2,128,768]{2,1,0:T(8,128)(2,1)S(1)} %bitcast.7, f32[1,768]{1,0:T(1,128)S(1)} %reshape.25.refs_2_, s32[1,1024]{1,0:T(1,128)S(1)} %bitcast.9, f32[2,1024]{1,0:T(2,128)S(1)} %copy-done.5, ...), custom_call_target="tpu_custom_call" | custom-call | flops 6000000000 | bytes 4000000 | tf_op jit(solution)/shard_map/pallas_call | solution.py:436
  89.0 0.6 slice_select_fusion
  89.7 0.7 copy.19
  (1 shorter events, 0.0 us)
Async XLA Ops:
  0.6 1.5 %copy-start.4 = (bf16[16,768]{1,0:T(8,128)(2,1)S(1)}, bf16[16,768]{1,0:T(8,128)(2,1)}, u32[]{:S(2)}) copy-start(bf16[16,768]{1,0:T(8,128)(2,1)} %refs_11_.1) | copy-start | bytes 73732
  1.4 0.7 copy-start.5
  2.1 0.7 copy-start.6
  2.8 1.0 %copy-start = (bf16[96,2304]{1,0:T(8,128)(2,1)S(1)}, bf16[96,2304]{1,0:T(8,128)(2,1)}, u32[]{:S(2)}) copy-start(bf16[96,2304]{1,0:T(8,128)(2,1)} %refs_9_.1) | copy-start | bytes 1327108
  3.9 1.0 %copy-start.1 = (bf16[2,4,32,768]{3,2,1,0:T(8,128)(2,1)S(1)}, bf16[2,4,32,768]{3,2,1,0:T(8,128)(2,1)}, u32[]{:S(2)}) copy-start(bf16[2,4,32,768]{3,2,1,0:T(8,128)(2,1)} %param.15) | copy-start | bytes 1179652
  4.8 0.9 %copy-start.2 = (bf16[4,32,768]{2,1,0:T(8,128)(2,1)S(1)}, bf16[4,32,768]{2,1,0:T(8,128)(2,1)}, u32[]{:S(2)}) copy-start(bf16[4,32,768]{2,1,0:T(8,128)(2,1)} %param.14) | copy-start | bytes 589828
  5.8 0.9 %copy-start.3 = (bf16[96,768]{1,0:T(8,128)(2,1)S(1)}, bf16[96,768]{1,0:T(8,128)(2,1)}, u32[]{:S(2)}) copy-start(bf16[96,768]{1,0:T(8,128)(2,1)} %refs_10_.1) | copy-start | bytes 442372
  6.7 0.9 copy-start.7
  7.6 0.9 copy-start.8
  8.5 0.8 copy-start.9
  9.3 0.7 copy-start.10
where the time goes:
time: 90.9 us; the launch traced here: 90.3 us
  Pallas kernels  78.4 us (86%)
  local copies, waits for them, and re-layouts  10 us (11%)
  between operations  1.32 us (1%)
    pallas_call x1, Pallas kernels, local(): pl.pallas_call(functools.partial(body, (n_gx, n_gy, n_pa, rows, cols, mod...  78.4 us
    unnamed x24, local copies, waits for them, and re-layouts  9.34 us

commit v1 on v0

v1 whole, which is shorter than its diff:
```python
import functools
import math

import jax
import jax.numpy as jnp
import numpy as np
from jax import lax
from jax.experimental import pallas as pl
from jax.experimental.pallas import tpu as pltpu
from jax.sharding import PartitionSpec as P

HEADS = 12
FQ = 128
CH = 3
RAD = 3
STEPS = 2
EPS = 1e-06
NOISE_COEF = 0.3
MESH = pl.DeviceIdType.MESH
FAR = -1e30
LANES = 128
PACKET = 16
VMEM_BYTES = 63 * 1024 * 1024
SIDES = [(dr, dc) for dc in (-1, 1) for dr in (-1, 0, 1)]
F32 = jnp.float32
BF16 = jnp.bfloat16


def side_rows(rows, width):
    return -(-(rows + 2 * width) * width // 8) * 8


def side_cells(rows, cols, width):
    held = side_rows(rows, width)
    places = []
    for first in (-width, cols):
        group = [(r, first + c) for r in range(-width, rows + width) for c in range(width)]
        places += group + [None] * (held - len(group))
    return places


def halo_cells(rows, cols, width):
    own = [(r, c) for r in range(rows) for c in range(cols)]
    above = [(r, c) for r in range(-width, 0) for c in range(cols)]
    below = [(r, c) for r in range(rows, rows + width) for c in range(cols)]
    return own + above + below + side_cells(rows, cols, width)


def packet_tables(rows, cols, width):
    places = side_cells(rows, cols, width)
    pick = np.zeros((len(SIDES) * PACKET, rows * cols), np.float32)
    put = np.zeros((len(places), len(SIDES) * PACKET), np.float32)
    for number, (dr, dc) in enumerate(SIDES):
        line = number * PACKET
        for place, cell in enumerate(places):
            if cell is None:
                continue
            r, c = cell[0] + dr * rows, cell[1] + dc * cols
            if 0 <= r < rows and 0 <= c < cols:
                pick[line, r * cols + c] = 1.0
                put[place, line] = 1.0
                line += 1
        assert line <= (number + 1) * PACKET
    return pick, put


def window_bias(rows, cols, width):
    cells = halo_cells(rows, cols, width)
    bias = np.full((len(cells), rows * cols), FAR, np.float32)
    for place, cell in enumerate(cells):
        if cell is None:
            continue
        for r in range(rows):
            for c in range(cols):
                if abs(cell[0] - r) <= width and abs(cell[1] - c) <= width:
                    bias[place, r * cols + c] = 0.0
    return bias


def sine_terms(t):
    z = (t * t) * (4.0 * math.pi * math.pi)
    odd = jnp.full_like(t, -1.0 / math.factorial(15))
    for power in range(13, 0, -2):
        odd = odd * z + (-1.0) ** (power // 2) / math.factorial(power)
    even = jnp.full_like(t, 1.0 / math.factorial(16))
    for power in range(14, -1, -2):
        even = even * z + (-1.0) ** (power // 2) / math.factorial(power)
    return odd * (t * (2.0 * math.pi)), even


def dot(a, b):
    return lax.dot_general(a, b, (((1,), (0,)), ((), ())), preferred_element_type=F32)


def dot_t(a, b):
    return lax.dot_general(a, b, (((1,), (1,)), ((), ())), preferred_element_type=F32)


def body(dims, gather, *refs):
    n_gx, n_gy, n_pa, rows, cols, model = dims
    loads, refs = refs[:11], refs[11:]
    weight_in, refs = refs[:4], refs[4:]
    out_ref, val_ref, *refs = refs
    staged, refs = refs[:11], refs[11:]
    (noise_ref, gain_ref, cell_ref, offset_ref, near_bias_ref, probe_bias_ref, near_pick_ref, near_put_ref,
     probe_pick_ref, probe_put_ref) = staged[1:]
    held0 = staged[0]
    if gather:
        weights, refs = refs[:6], refs[6:]
        head_s, w_send, w_recv, w_here, *refs = refs
    (held1, held2, got0, got1, got2, pack0, pack1, pack2, h_send, h_recv, l_sem, normed, q_s, kv_s, att_s,
     hot_s, feat_s, qt_s, ut_s) = refs
    held, got, pack = (held0, held1, held2), (got0, got1, got2), (pack0, pack1, pack2)
    own = rows * cols
    gx, gy, pa = lax.axis_index("gx"), lax.axis_index("gy"), lax.axis_index("pa")
    ring = n_gx * n_pa
    place = gx * n_pa + pa

    local_copies = []
    for number, source in enumerate(loads):
        target = held0.at[pl.ds(0, own)] if number == 0 else staged[number]
        local_copies.append(pltpu.make_async_copy(source, target, l_sem.at[number]))
        local_copies[-1].start()

    def device(dr, dc):
        r = lax.rem(place + dr + ring, ring)
        return (lax.div(r, n_pa), lax.rem(gy + dc + n_gy, n_gy), lax.rem(r, n_pa))

    around = [device(-1, 0), device(1, 0)] + [device(dr, dc) for dr, dc in SIDES]
    partners = list(around)
    if gather:
        pa_x = lax.rem(pa + 2, 4)
        to_x, to_y = (gx, gy, pa_x), (1 - gx, gy, pa)
        to_twin = (gx, gy, pa + 1 - 2 * lax.rem(pa, 2))
        partners += [to_x, to_y, to_twin]
    barrier = pltpu.get_barrier_semaphore()
    for target in partners:
        pl.semaphore_signal(barrier, inc=1, device_id=target, device_id_type=MESH)
    pl.semaphore_wait(barrier, len(partners))

    started = []

    def push(src, dst, send, recv, target):
        copy = pltpu.make_async_remote_copy(
            src_ref=src, dst_ref=dst, send_sem=send, recv_sem=recv, device_id=target, device_id_type=MESH
        )
        copy.start()
        started.append(copy)
        return copy

    def widths(number):
        return RAD if number < STEPS else 1

    def halo_start(number):
        width = widths(number)
        span = width * cols
        here, send, recv = held[number], h_send.at[number], h_recv.at[number]
        copies = [
            push(here.at[pl.ds(0, span)], here.at[pl.ds(own + span, span)], send.at[0], recv.at[0], around[0]),
            push(here.at[pl.ds(own - span, span)], here.at[pl.ds(own, span)], send.at[1], recv.at[1], around[1]),
        ]
        pick = near_pick_ref if number < STEPS else probe_pick_ref
        pack[number][...] = dot(pick[...], here[pl.ds(0, own)]).astype(BF16)
        for k in range(len(SIDES)):
            part = pl.ds(k * PACKET, PACKET)
            copies.append(
                push(pack[number].at[part], got[number].at[part], send.at[2 + k], recv.at[2 + k], around[2 + k])
            )
        return copies

    def halo_end(number, copies):
        for copy in copies:
            copy.wait_recv()
        put = near_put_ref if number < STEPS else probe_put_ref
        base = own + 2 * widths(number) * cols
        held[number][pl.ds(base, put.shape[0])] = dot(put[...], got[number][...]).astype(BF16)

    class Moves:
        def __init__(self, number, source):
            self.number, self.ref, self.source = number, weights[number], source
            half = self.ref.shape[1] // 2
            self.cut = half if half % 16 == 0 else None
            self.slot = {}

        def send(self, slot, src, dst, target):
            self.slot[slot] = push(src, dst, w_send.at[self.number, slot], w_recv.at[self.number, slot], target)

        def go(self, slot, part, target, lo=None, size=None):
            view = self.ref.at[part] if lo is None else self.ref.at[part, pl.ds(lo, size)]
            self.send(slot, view, view, target)

        def begin(self):
            here = self.ref.at[place]
            self.send(0, self.source, here, to_x)
            self.send(1, self.source, here, to_y)
            self.send(2, self.source, here, to_twin)

        def middle(self):
            near_x, near_y = gx * 4 + pa_x, (1 - gx) * 4 + pa
            self.slot[0].wait_recv()
            if self.cut is None:
                self.go(3, near_x, to_y)
            else:
                self.go(3, near_x, to_y, 0, self.cut)
            self.go(5, near_x, to_twin)
            self.slot[1].wait_recv()
            if self.cut is not None:
                self.go(4, near_y, to_x, self.cut, self.cut)
            self.go(6, near_y, to_twin)

        def end(self):
            across = (1 - gx) * 4 + pa_x
            self.slot[3].wait_recv()
            if self.cut is None:
                self.go(7, across, to_twin)
            else:
                self.go(7, across, to_twin, 0, self.cut)
                self.slot[4].wait_recv()
                self.go(8, across, to_twin, self.cut, self.cut)

        def finish(self):
            for slot in (2, 5, 6, 7, 8):
                if slot in self.slot:
                    self.slot[slot].wait_recv()

    tile = 256
    pairs = model // LANES
    keys = kv_s.shape[0]
    half = LANES // 2
    slots = cell_ref.shape[1]
    scale = math.log2(math.e) / math.sqrt(model // HEADS)

    if gather:
        sources = [weight_in[0].at[:, pl.ds(i * model, model)] for i in range(3)] + [weight_in[1], weight_in[2]]
        here_copies = [
            pltpu.make_async_copy(source, weights[i].at[place], w_here.at[i]) for i, source in enumerate(sources)
        ]
        here_copies.append(pltpu.make_async_copy(weight_in[3], head_s, w_here.at[5]))
        move_q, move_k, move_v, move_out, move_query = [Moves(i, source) for i, source in enumerate(sources)]
        move_head = Moves(5, weights[5].at[place])
        move_k.begin()
        move_q.begin()
        for copy in here_copies:
            copy.start()

    for copy in local_copies:
        copy.wait()
    halo = halo_start(0)

    cells = lax.broadcasted_iota(jnp.int32, (own, slots), 0)
    hot_s[...] = jnp.where(cells == cell_ref[...], 1.0, 0.0).astype(BF16)
    quarter = FQ // 4
    freq = lax.broadcasted_iota(jnp.int32, (quarter, slots), 0).astype(F32) + 1.0
    for axis in range(2):
        turns = freq * offset_ref[pl.ds(axis, 1), :]
        sine, cosine = sine_terms(turns - jnp.floor(turns + 0.5))
        feat_s[pl.ds(2 * axis * quarter, quarter)] = sine.astype(BF16)
        feat_s[pl.ds((2 * axis + 1) * quarter, quarter)] = cosine.astype(BF16)
    if gather:
        for copy in here_copies:
            copy.wait()
        weights[5][place] = jnp.zeros(weights[5].shape[1:], BF16)
        weights[5][place, 0:CH, 0 : model // ring] = head_s[...]

    def normalize(number, lo, count):
        part = pl.ds(lo, count)
        values = held[number][part].astype(F32)
        factor = lax.rsqrt(jnp.mean(values * values, axis=-1, keepdims=True) + EPS)
        normed[part] = (values * factor * gain_ref[...].reshape(1, model)).astype(BF16)

    def columns(piece, start, size):
        if gather:
            return weights[piece][:, :, pl.ds(start, size)].reshape(model, size)
        if piece < 3:
            return weight_in[0][:, pl.ds(piece * model + start, size)]
        return weight_in[piece - 2][:, pl.ds(start, size)]

    def project(piece, lo, count):
        def block(i, carry):
            start = pl.multiple_of(i * tile, tile)
            made = dot(normed[pl.ds(lo, count)], columns(piece, start, tile))
            if piece == 0:
                q_s[pl.ds(lo, count), pl.ds(start, tile)] = (made * scale).astype(BF16)
            else:
                kv_s[pl.ds(lo, count), pl.ds((piece - 1) * model + start, tile)] = made.astype(BF16)
            return carry

        lax.fori_loop(0, model // tile, block, 0)

    def attend():
        lane = lax.broadcasted_iota(jnp.int32, (own, LANES), 1)
        low = lane < half
        unit = jnp.where(lane == lax.broadcasted_iota(jnp.int32, (own, LANES), 0), 1.0, 0.0).astype(BF16)
        zero = jnp.zeros((own, LANES), BF16)
        ones = jnp.ones((keys, LANES), BF16)

        def pair(i, carry):
            start = pl.multiple_of(i * LANES, LANES)
            query = q_s[:, pl.ds(start, LANES)]
            both = jnp.concatenate(
                [
                    jnp.concatenate([unit, jnp.where(low, query, zero)], axis=1),
                    jnp.concatenate([unit, jnp.where(low, zero, query)], axis=1),
                ],
                axis=0,
            )
            key = jnp.concatenate([near_bias_ref[...], kv_s[:, pl.ds(start, LANES)]], axis=1)
            scores = dot_t(both, key)
            top = jnp.max(scores, axis=1, keepdims=True)
            weight = jnp.exp2(scores - top).astype(BF16)
            value = jnp.concatenate(
                [kv_s[:, pl.ds(pl.multiple_of(model + start, LANES), LANES)], ones], axis=1
            )
            mixed = dot(weight, value)
            mixed = mixed[:, :LANES] / mixed[:, LANES:]
            att_s[:, pl.ds(start, LANES)] = jnp.where(low, mixed[:own], mixed[own:]).astype(BF16)
            return carry

        lax.fori_loop(0, pairs, pair, 0, unroll=2)

    def update(step):
        for start in range(0, model, tile):
            cut = pl.ds(start, tile)
            moved = dot(att_s[...], columns(3, start, tile))
            held[step + 1][pl.ds(0, own), cut] = (
                held[step][pl.ds(0, own), cut].astype(F32)
                + moved / STEPS
                + NOISE_COEF * noise_ref[step, :, cut].astype(F32)
            ).astype(BF16)

    if gather:
        move_k.middle()
        move_v.begin()
    halo_end(0, halo)
    normalize(0, 0, keys)
    if gather:
        move_q.middle()
        move_out.begin()
        move_k.end()
        move_v.middle()
        move_query.begin()
        move_head.begin()
        move_q.end()
        move_k.finish()
    project(1, 0, keys)
    if gather:
        move_out.middle()
        move_v.end()
        move_q.finish()
    project(0, 0, own)
    if gather:
        move_query.middle()
        move_head.middle()
        move_out.end()
        move_v.finish()
    project(2, 0, keys)
    attend()
    if gather:
        move_query.end()
        move_head.end()
        move_out.finish()
    update(0)
    halo = halo_start(1)
    normalize(1, 0, own)
    for piece in range(3):
        project(piece, 0, own)
    if gather:
        move_query.finish()
        move_head.finish()
    turned = (
        weights[4][...].reshape(FQ, model) if gather else weight_in[2][...]
    )
    turned = turned.astype(F32).T.astype(BF16)
    for start in range(0, slots, tile):
        qt_s[:, pl.ds(start, tile)] = (dot(turned, feat_s[:, pl.ds(start, tile)]) * scale).astype(BF16)
    halo_end(1, halo)
    normalize(1, own, keys - own)
    project(1, own, keys - own)
    project(2, own, keys - own)
    attend()
    update(1)
    halo = halo_start(2)
    out_ref[...] = held2[pl.ds(0, own)]
    if gather:
        head = jnp.concatenate([weights[5][j, :, 0 : model // ring] for j in range(ring)], axis=1)
    else:
        head = weight_in[3][...]
    every = jnp.concatenate([head.astype(F32)] * HEADS, axis=0)
    line = lax.broadcasted_iota(jnp.int32, every.shape, 0) // 16
    owner = lax.broadcasted_iota(jnp.int32, every.shape, 1) // (model // HEADS)
    every = jnp.where(line == owner, every, 0.0).astype(BF16)
    val_ref[...] = jnp.zeros_like(val_ref)
    halo_end(2, halo)
    near = held2.shape[0]
    turned = dot_t(every, held2[...])
    line = lax.rem(lax.broadcasted_iota(jnp.int32, turned.shape, 0), 16)
    ut_s[...] = jnp.where(line == CH, 1.0, turned).astype(BF16).reshape(HEADS, 16, near)

    def decode(i, carry):
        start = pl.multiple_of(i * LANES, LANES)
        key = jnp.concatenate([probe_bias_ref[...], held2[:, pl.ds(start, LANES)]], axis=1)
        for first in range(0, slots, tile):
            cut = pl.ds(first, tile)
            hot = hot_s[:, cut]
            blank = jnp.zeros((half, tile), BF16)
            total = val_ref[:, cut]
            for side in range(2):
                query = qt_s[pl.ds(pl.multiple_of(start + side * half, half), half), cut]
                parts = [hot, query, blank] if side == 0 else [hot, blank, query]
                scores = dot(key, jnp.concatenate(parts, axis=0))
                top = jnp.max(scores, axis=0, keepdims=True)
                weight = jnp.exp2(scores - top).astype(BF16)
                mixed = dot(ut_s[2 * i + side], weight)
                total = total + mixed[0:8] / mixed[CH : CH + 1]
            val_ref[:, cut] = total
        return carry

    lax.fori_loop(0, pairs, decode, 0)
    for copy in started:
        copy.wait_send()


def local(sizes, latents, noise, proc_gain, w_qkv, w_out, w_query, w_head, probe_cell, probe_offset, probe_count):
    n_gx, n_gy, n_pa = sizes
    rows, cols, model = latents.shape
    own = rows * cols
    slots = probe_cell.shape[0]
    shards = [w_qkv, w_out, w_query, w_head]
    gather = n_gx == 2 and n_pa == 4 and all(shard.shape[0] % 16 == 0 for shard in shards)
    count = n_gx * n_pa
    if not gather:
        shards = [lax.all_gather(shard, ("gx", "pa"), axis=0, tiled=True) for shard in shards]
        shards[3] = jnp.pad(shards[3].T, ((0, 16 - CH), (0, 0)))
    else:
        shards[3] = w_head.T
    near = len(halo_cells(rows, cols, RAD))
    close = len(halo_cells(rows, cols, 1))
    tables = [
        jnp.asarray(table, BF16)
        for table in (
            window_bias(rows, cols, RAD),
            window_bias(rows, cols, 1),
            *packet_tables(rows, cols, RAD),
            *packet_tables(rows, cols, 1),
        )
    ]
    loads = [
        latents.reshape(own, model),
        noise.reshape(STEPS, own, model),
        proc_gain,
        probe_cell.reshape(1, slots),
        probe_offset,
        *tables,
    ]
    scratch = [pltpu.VMEM((near, model), BF16)] + [pltpu.VMEM(load.shape, load.dtype) for load in loads[1:]]
    if gather:
        block = (count, w_out.shape[0], model)
        scratch += [pltpu.VMEM(block, BF16)] * 4
        scratch += [pltpu.VMEM((count,) + w_query.shape, BF16), pltpu.VMEM((count, 16, LANES), BF16)]
        scratch += [pltpu.VMEM(shards[3].shape, BF16)]
        scratch += [pltpu.SemaphoreType.DMA((6, 9)), pltpu.SemaphoreType.DMA((6, 9)), pltpu.SemaphoreType.DMA((6,))]
    scratch += [pltpu.VMEM((size, model), BF16) for size in (near, close)]
    scratch += [pltpu.VMEM((len(SIDES) * PACKET, model), BF16)] * 6
    scratch += [pltpu.SemaphoreType.DMA((STEPS + 1, 8)), pltpu.SemaphoreType.DMA((STEPS + 1, 8))]
    scratch += [pltpu.SemaphoreType.DMA((len(loads),))]
    scratch += [
        pltpu.VMEM((near, model), BF16),
        pltpu.VMEM((own, model), BF16),
        pltpu.VMEM((near, 2 * model), BF16),
        pltpu.VMEM((own, model), BF16),
        pltpu.VMEM((own, slots), BF16),
        pltpu.VMEM((FQ, slots), BF16),
        pltpu.VMEM((model, slots), BF16),
        pltpu.VMEM((HEADS, 16, close), BF16),
    ]
    apart = pl.BlockSpec(memory_space=pltpu.HBM)
    inside = pl.BlockSpec(memory_space=pltpu.VMEM)
    latent_out, values = pl.pallas_call(
        functools.partial(body, (n_gx, n_gy, n_pa, rows, cols, model), gather),
        out_shape=(jax.ShapeDtypeStruct((own, model), BF16), jax.ShapeDtypeStruct((8, slots), F32)),
        in_specs=[apart] * len(loads) + [apart if gather else inside] * len(shards),
        out_specs=[inside] * 2,
        scratch_shapes=scratch,
        compiler_params=pltpu.CompilerParams(
            collective_id=0, has_side_effects=True, vmem_limit_bytes=VMEM_BYTES
        ),
        cost_estimate=pl.CostEstimate(flops=6_000_000_000, bytes_accessed=4_000_000, transcendentals=4_000_000),
    )(*loads, *shards)
    live = jnp.arange(slots, dtype=jnp.int32) < probe_count[0]
    probe_values = jnp.where(live[None, :], values[:CH], jnp.zeros((), F32))
    return (latent_out.reshape(rows, cols, model), probe_values)


def solution(mesh):
    sizes = (mesh.shape["gx"], mesh.shape["gy"], mesh.shape["pa"])
    return jax.shard_map(
        functools.partial(local, sizes),
        mesh=mesh,
        in_specs=(
            P(("gx", "pa"), "gy", None),
            P(None, ("gx", "pa"), "gy", None),
            P(),
            P(("gx", "pa"), None),
            P(("gx", "pa"), None),
            P(("gx", "pa"), None),
            P(("gx", "pa"), None),
            P(("gx", "gy", "pa")),
            P(None, ("gx", "gy", "pa")),
            P(("gx", "gy", "pa")),
        ),
        out_specs=(P(("gx", "pa"), "gy", None), P(None, ("gx", "gy", "pa"))),
        check_vma=False,
    )
```

time: 90.9 us -> 70.2 us (0.77)
  Pallas kernels: 78.4 us -> 65.7 us
  local copies, waits for them, and re-layouts: 10 us -> 1.62 us
    pallas_call x1, Pallas kernels: 78.4 us -> 65.7 us  [local(): pl.pallas_call(functools.partial(body, (n_gx, n_gy, n_pa, rows, cols, mod...]
    unnamed x24 -> x1, local copies, waits for them, and re-layouts: 9.34 us -> 1.62 us
where the time goes in v1:
time: 70.2 us; the launch traced here: 70 us
  Pallas kernels  65.7 us (94%)
  local copies, waits for them, and re-layouts  1.62 us (2%)
  other arithmetic  1.38 us (2%)
  between operations  1.3 us (2%)
    pallas_call x1, Pallas kernels, local(): pl.pallas_call(functools.partial(body, (n_gx, n_gy, n_pa, rows, cols, mod...  65.7 us
    unnamed x1, local copies, waits for them, and re-layouts  1.62 us

profile of v1, /device:TPU:0, one launch (start us, length us, event | category | flops | bytes accessed | tf_op | source)
XLA Modules:
  0.0 70.0 jit_solution(1210300000171646587)
XLA Ops:
  0.6 65.7 %shard_map.167 = (bf16[128,768]{1,0:T(8,128)(2,1)}, f32[8,1024]{1,0:T(8,128)}) custom-call(bf16[128,768]{1,0:T(8,128)(2,1)} %bitcast.9, bf16[2,128,768]{2,1,0:T(8,128)(2,1)} %bitcast.8, f32[768]{0:T(1024)} %refs_2_.1, s32[1,1024]{1,0:T(1,128)} %bitcast.10, f32[2,1024]{1,0:T(2,128)} %refs_4_.1, bf16[384,128]{1,0:T(8,128)(2,1)} %constant.14.clone.refs_5_, ...), custom_call_target="tpu_custom_call" | custom-call | flops 6000000000 | bytes 4000000 | tf_op jit(solution)/shard_map/pallas_call | solution.py:478
  67.0 1.4 %slice_select_fusion = f32[3,1024]{1,0:T(4,128)} fusion(f32[8,1024]{1,0:T(8,128)} %get-tuple-element.5, pred[1024]{0:T(1024)(128)(4,1)S(1)} %iota_compare_fusion), kind=kLoop, calls=%fused_computation | loop fusion | flops 3072 | bytes 25600 | tf_op jit(solution)/shard_map/jit(_where)/select_n | solution.py:490
  68.4 1.6 %copy.20 = bf16[4,32,768]{2,1,0:T(8,128)(2,1)} copy(bf16[4,32,768]{2,1,0:T(8,128)(2,1)} %bitcast.7) | data formatting | bytes 393216
  (1 shorter events, 0.0 us)

commit v2 on v1

--- a/solution.py
+++ b/solution.py
@@ -20,7 +20,7 @@
 FAR = -1e30
 LANES = 128
 PACKET = 16
-VMEM_BYTES = 63 * 1024 * 1024
+VMEM_BYTES = 61 * 1024 * 1024
 SIDES = [(dr, dc) for dc in (-1, 1) for dr in (-1, 0, 1)]
 F32 = jnp.float32
 BF16 = jnp.bfloat16
@@ -238,10 +238,15 @@
         here_copies.append(pltpu.make_async_copy(weight_in[3], head_s, w_here.at[5]))
         move_q, move_k, move_v, move_out, move_query = [Moves(i, source) for i, source in enumerate(sources)]
         move_head = Moves(5, weights[5].at[place])
+        for copy in here_copies[::-1]:
+            copy.start()
+        move_query.begin()
         move_k.begin()
         move_q.begin()
-        for copy in here_copies:
-            copy.start()
+        here_copies[5].wait()
+        weights[5][place] = jnp.zeros(weights[5].shape[1:], BF16)
+        weights[5][place, 0:CH, 0 : model // ring] = head_s[...]
+        move_head.begin()
 
     for copy in local_copies:
         copy.wait()
@@ -257,10 +262,10 @@
         feat_s[pl.ds(2 * axis * quarter, quarter)] = sine.astype(BF16)
         feat_s[pl.ds((2 * axis + 1) * quarter, quarter)] = cosine.astype(BF16)
     if gather:
-        for copy in here_copies:
+        move_query.middle()
+        move_head.middle()
+        for copy in here_copies[:5]:
             copy.wait()
-        weights[5][place] = jnp.zeros(weights[5].shape[1:], BF16)
-        weights[5][place, 0:CH, 0 : model // ring] = head_s[...]
 
     def normalize(number, lo, count):
         part = pl.ds(lo, count)
@@ -285,7 +290,7 @@
                 kv_s[pl.ds(lo, count), pl.ds((piece - 1) * model + start, tile)] = made.astype(BF16)
             return carry
 
-        lax.fori_loop(0, model // tile, block, 0)
+        lax.fori_loop(0, model // tile, block, 0, unroll=True)
 
     def attend():
         lane = lax.broadcasted_iota(jnp.int32, (own, LANES), 1)
@@ -316,7 +321,7 @@
             att_s[:, pl.ds(start, LANES)] = jnp.where(low, mixed[:own], mixed[own:]).astype(BF16)
             return carry
 
-        lax.fori_loop(0, pairs, pair, 0, unroll=2)
+        lax.fori_loop(0, pairs, pair, 0, unroll=3 if pairs % 3 == 0 else 1)
 
     def update(step):
         for start in range(0, model, tile):
@@ -328,51 +333,44 @@
                 + NOISE_COEF * noise_ref[step, :, cut].astype(F32)
             ).astype(BF16)
 
-    if gather:
+    halo_end(0, halo)
+    normalize(0, 0, keys)
+    if gather:
+        move_query.end()
+        move_head.end()
         move_k.middle()
         move_v.begin()
-    halo_end(0, halo)
-    normalize(0, 0, keys)
+        move_query.finish()
+        move_head.finish()
+    turned = weights[4][...].reshape(FQ, model) if gather else weight_in[2][...]
+    turned = turned.astype(F32).T.astype(BF16)
+    for start in range(0, slots, tile):
+        qt_s[:, pl.ds(start, tile)] = (dot(turned, feat_s[:, pl.ds(start, tile)]) * scale).astype(BF16)
     if gather:
         move_q.middle()
-        move_out.begin()
         move_k.end()
         move_v.middle()
-        move_query.begin()
-        move_head.begin()
+        move_out.begin()
         move_q.end()
         move_k.finish()
     project(1, 0, keys)
     if gather:
-        move_out.middle()
-        move_v.end()
         move_q.finish()
     project(0, 0, own)
     if gather:
-        move_query.middle()
-        move_head.middle()
-        move_out.end()
+        move_v.end()
+        move_out.middle()
         move_v.finish()
     project(2, 0, keys)
     attend()
     if gather:
-        move_query.end()
-        move_head.end()
+        move_out.end()
         move_out.finish()
     update(0)
     halo = halo_start(1)
     normalize(1, 0, own)
     for piece in range(3):
         project(piece, 0, own)
-    if gather:
-        move_query.finish()
-        move_head.finish()
-    turned = (
-        weights[4][...].reshape(FQ, model) if gather else weight_in[2][...]
-    )
-    turned = turned.astype(F32).T.astype(BF16)
-    for start in range(0, slots, tile):
-        qt_s[:, pl.ds(start, tile)] = (dot(turned, feat_s[:, pl.ds(start, tile)]) * scale).astype(BF16)
     halo_end(1, halo)
     normalize(1, own, keys - own)
     project(1, own, keys - own)
@@ -398,18 +396,24 @@
 
     def decode(i, carry):
         start = pl.multiple_of(i * LANES, LANES)
-        key = jnp.concatenate([probe_bias_ref[...], held2[:, pl.ds(start, LANES)]], axis=1)
+        context = held2[:, pl.ds(start, LANES)]
+        low = lax.broadcasted_iota(jnp.int32, context.shape, 1) < half
+        blank = jnp.zeros_like(context)
+        key = jnp.concatenate(
+            [
+                jnp.concatenate([probe_bias_ref[...], jnp.where(low, context, blank)], axis=1),
+                jnp.concatenate([probe_bias_ref[...], jnp.where(low, blank, context)], axis=1),
+            ],
+            axis=0,
+        )
         for first in range(0, slots, tile):
             cut = pl.ds(first, tile)
-            hot = hot_s[:, cut]
-            blank = jnp.zeros((half, tile), BF16)
+            scores = dot(key, jnp.concatenate([hot_s[:, cut], qt_s[pl.ds(start, LANES), cut]], axis=0))
             total = val_ref[:, cut]
             for side in range(2):
-                query = qt_s[pl.ds(pl.multiple_of(start + side * half, half), half), cut]
-                parts = [hot, query, blank] if side == 0 else [hot, blank, query]
-                scores = dot(key, jnp.concatenate(parts, axis=0))
-                top = jnp.max(scores, axis=0, keepdims=True)
-                weight = jnp.exp2(scores - top).astype(BF16)
+                part = scores[side * near : (side + 1) * near]
+                top = jnp.max(part, axis=0, keepdims=True)
+                weight = jnp.exp2(part - top).astype(BF16)
                 mixed = dot(ut_s[2 * i + side], weight)
                 total = total + mixed[0:8] / mixed[CH : CH + 1]
             val_ref[:, cut] = total

time: 70.2 us -> 66.7 us (0.950)
  Pallas kernels: 65.7 us -> 62.2 us
    pallas_call x1, Pallas kernels: 65.7 us -> 62.2 us  [local(): pl.pallas_call(functools.partial(body, (n_gx, n_gy, n_pa, rows, cols, mod...]
where the time goes in v2:
time: 66.7 us; the launch traced here: 66.5 us
  Pallas kernels  62.2 us (93%)
  local copies, waits for them, and re-layouts  1.62 us (2%)
  other arithmetic  1.38 us (2%)
  between operations  1.3 us (2%)
    pallas_call x1, Pallas kernels, local(): pl.pallas_call(functools.partial(body, (n_gx, n_gy, n_pa, rows, cols, mod...  62.2 us
    unnamed x1, local copies, waits for them, and re-layouts  1.62 us
    select_n x1, other arithmetic, local(): probe_values = jnp.where(live[None, :], values[:CH], jnp.zeros((), F32))  1.37 us

profile of v2, /device:TPU:0, one launch (start us, length us, event | category | flops | bytes accessed | tf_op | source)
XLA Modules:
  0.0 66.5 jit_solution(199254317770368120)
XLA Ops:
  0.6 62.2 %shard_map.167 = (bf16[128,768]{1,0:T(8,128)(2,1)}, f32[8,1024]{1,0:T(8,128)}) custom-call(bf16[128,768]{1,0:T(8,128)(2,1)} %bitcast.9, bf16[2,128,768]{2,1,0:T(8,128)(2,1)} %bitcast.8, f32[768]{0:T(1024)} %refs_2_.1, s32[1,1024]{1,0:T(1,128)} %bitcast.10, f32[2,1024]{1,0:T(2,128)} %refs_4_.1, bf16[384,128]{1,0:T(8,128)(2,1)} %constant.14.clone.refs_5_, ...), custom_call_target="tpu_custom_call" | custom-call | flops 6000000000 | bytes 4000000 | tf_op jit(solution)/shard_map/pallas_call | solution.py:482
  63.5 1.4 %slice_select_fusion = f32[3,1024]{1,0:T(4,128)} fusion(f32[8,1024]{1,0:T(8,128)} %get-tuple-element.5, pred[1024]{0:T(1024)(128)(4,1)S(1)} %iota_compare_fusion), kind=kLoop, calls=%fused_computation | loop fusion | flops 3072 | bytes 25600 | tf_op jit(solution)/shard_map/jit(_where)/select_n | solution.py:494
  64.8 1.6 %copy.20 = bf16[4,32,768]{2,1,0:T(8,128)(2,1)} copy(bf16[4,32,768]{2,1,0:T(8,128)(2,1)} %bitcast.7) | data formatting | bytes 393216
  (1 shorter events, 0.0 us)

commit v3 on v2

--- a/solution.py
+++ b/solution.py
@@ -109,7 +109,7 @@
         weights, refs = refs[:6], refs[6:]
         head_s, w_send, w_recv, w_here, *refs = refs
     (held1, held2, got0, got1, got2, pack0, pack1, pack2, h_send, h_recv, l_sem, normed, q_s, kv_s, att_s,
-     hot_s, feat_s, qt_s, ut_s) = refs
+     hot_s, feat_s, qt_s, ut_s, part_s, out_sem) = refs
     held, got, pack = (held0, held1, held2), (got0, got1, got2), (pack0, pack1, pack2)
     own = rows * cols
     gx, gy, pa = lax.axis_index("gx"), lax.axis_index("gy"), lax.axis_index("pa")
@@ -378,7 +378,8 @@
     attend()
     update(1)
     halo = halo_start(2)
-    out_ref[...] = held2[pl.ds(0, own)]
+    leave = pltpu.make_async_copy(held2.at[pl.ds(0, own)], out_ref, out_sem.at[0])
+    leave.start()
     if gather:
         head = jnp.concatenate([weights[5][j, :, 0 : model // ring] for j in range(ring)], axis=1)
     else:
@@ -387,41 +388,65 @@
     line = lax.broadcasted_iota(jnp.int32, every.shape, 0) // 16
     owner = lax.broadcasted_iota(jnp.int32, every.shape, 1) // (model // HEADS)
     every = jnp.where(line == owner, every, 0.0).astype(BF16)
+
+    def decode(lo, count, last):
+        part = pl.ds(lo, count)
+        turned = dot_t(every, held2[part])
+        line = lax.rem(lax.broadcasted_iota(jnp.int32, turned.shape, 0), 16)
+        ut_s[:, :, 0:count] = jnp.where(line == CH, 1.0, turned).astype(BF16).reshape(HEADS, 16, count)
+
+        def pair(i, carry):
+            start = pl.multiple_of(i * LANES, LANES)
+            context = held2[part, pl.ds(start, LANES)]
+            bias = probe_bias_ref[part]
+            low = lax.broadcasted_iota(jnp.int32, context.shape, 1) < half
+            blank = jnp.zeros_like(context)
+            key = jnp.concatenate(
+                [
+                    jnp.concatenate([bias, jnp.where(low, context, blank)], axis=1),
+                    jnp.concatenate([bias, jnp.where(low, blank, context)], axis=1),
+                ],
+                axis=0,
+            )
+            for first in range(0, slots, tile):
+                cut = pl.ds(first, tile)
+                scores = dot(key, jnp.concatenate([hot_s[:, cut], qt_s[pl.ds(start, LANES), cut]], axis=0))
+                total = val_ref[:, cut] if last else None
+                for side in range(2):
+                    some = scores[side * count : (side + 1) * count]
+                    top = jnp.max(some, axis=0, keepdims=True)
+                    weight = jnp.exp2(some - top).astype(BF16)
+                    mixed = dot(ut_s[2 * i + side, :, 0:count], weight)[0:8]
+                    if not last:
+                        place_in = lax.broadcasted_iota(jnp.int32, mixed.shape, 0)
+                        part_s[2 * i + side, :, cut] = jnp.where(place_in == CH + 1, top, mixed)
+                        continue
+                    early = part_s[2 * i + side, :, cut]
+                    early_top = early[CH + 1 : CH + 2]
+                    both = jnp.maximum(early_top, top)
+                    mixed = early * jnp.exp2(early_top - both) + mixed * jnp.exp2(top - both)
+                    total = total + mixed / mixed[CH : CH + 1]
+                if last:
+                    val_ref[:, cut] = total
+            return carry
+
+        lax.fori_loop(0, pairs, pair, 0)
+
     val_ref[...] = jnp.zeros_like(val_ref)
+    decode(0, own, False)
     halo_end(2, halo)
-    near = held2.shape[0]
-    turned = dot_t(every, held2[...])
-    line = lax.rem(lax.broadcasted_iota(jnp.int32, turned.shape, 0), 16)
-    ut_s[...] = jnp.where(line == CH, 1.0, turned).astype(BF16).reshape(HEADS, 16, near)
-
-    def decode(i, carry):
-        start = pl.multiple_of(i * LANES, LANES)
-        context = held2[:, pl.ds(start, LANES)]
-        low = lax.broadcasted_iota(jnp.int32, context.shape, 1) < half
-        blank = jnp.zeros_like(context)
-        key = jnp.concatenate(
-            [
-                jnp.concatenate([probe_bias_ref[...], jnp.where(low, context, blank)], axis=1),
-                jnp.concatenate([probe_bias_ref[...], jnp.where(low, blank, context)], axis=1),
-            ],
-            axis=0,
-        )
-        for first in range(0, slots, tile):
-            cut = pl.ds(first, tile)
-            scores = dot(key, jnp.concatenate([hot_s[:, cut], qt_s[pl.ds(start, LANES), cut]], axis=0))
-            total = val_ref[:, cut]
-            for side in range(2):
-                part = scores[side * near : (side + 1) * near]
-                top = jnp.max(part, axis=0, keepdims=True)
-                weight = jnp.exp2(part - top).astype(BF16)
-                mixed = dot(ut_s[2 * i + side], weight)
-                total = total + mixed[0:8] / mixed[CH : CH + 1]
-            val_ref[:, cut] = total
-        return carry
-
-    lax.fori_loop(0, pairs, decode, 0)
+    decode(own, held2.shape[0] - own, True)
+    leave.wait()
     for copy in started:
         copy.wait_send()
+
+
+def finish(count_ref, latent_ref, value_ref, out_ref, val_ref, sem):
+    copy = pltpu.make_async_copy(latent_ref, out_ref, sem.at[0])
+    copy.start()
+    slot = lax.broadcasted_iota(jnp.int32, val_ref.shape, 1)
+    val_ref[...] = jnp.where(slot < count_ref[0], value_ref[0:CH], 0.0)
+    copy.wait()
 
 
 def local(sizes, latents, noise, proc_gain, w_qkv, w_out, w_query, w_head, probe_cell, probe_offset, probe_count):
@@ -475,7 +500,9 @@
         pltpu.VMEM((own, slots), BF16),
         pltpu.VMEM((FQ, slots), BF16),
         pltpu.VMEM((model, slots), BF16),
-        pltpu.VMEM((HEADS, 16, close), BF16),
+        pltpu.VMEM((HEADS, 16, LANES), BF16),
+        pltpu.VMEM((HEADS, 8, slots), F32),
+        pltpu.SemaphoreType.DMA((1,)),
     ]
     apart = pl.BlockSpec(memory_space=pltpu.HBM)
     inside = pl.BlockSpec(memory_space=pltpu.VMEM)
@@ -483,15 +510,21 @@
         functools.partial(body, (n_gx, n_gy, n_pa, rows, cols, model), gather),
         out_shape=(jax.ShapeDtypeStruct((own, model), BF16), jax.ShapeDtypeStruct((8, slots), F32)),
         in_specs=[apart] * len(loads) + [apart if gather else inside] * len(shards),
-        out_specs=[inside] * 2,
+        out_specs=[apart, inside],
         scratch_shapes=scratch,
         compiler_params=pltpu.CompilerParams(
             collective_id=0, has_side_effects=True, vmem_limit_bytes=VMEM_BYTES
         ),
         cost_estimate=pl.CostEstimate(flops=6_000_000_000, bytes_accessed=4_000_000, transcendentals=4_000_000),
     )(*loads, *shards)
-    live = jnp.arange(slots, dtype=jnp.int32) < probe_count[0]
-    probe_values = jnp.where(live[None, :], values[:CH], jnp.zeros((), F32))
+    latent_out, probe_values = pl.pallas_call(
+        finish,
+        out_shape=(jax.ShapeDtypeStruct((own, model), BF16), jax.ShapeDtypeStruct((CH, slots), F32)),
+        in_specs=[pl.BlockSpec(memory_space=pltpu.SMEM), apart, inside],
+        out_specs=[apart, inside],
+        scratch_shapes=[pltpu.SemaphoreType.DMA((1,))],
+        compiler_params=pltpu.CompilerParams(vmem_limit_bytes=VMEM_BYTES),
+    )(probe_count, latent_out, values)
     return (latent_out.reshape(rows, cols, model), probe_values)
 
 

time: 66.7 us -> 71.4 us (1.070)
  Pallas kernels: 62.2 us -> 69.9 us
  local copies, waits for them, and re-layouts: 1.62 us -> 0 us
  other arithmetic: 1.38 us -> 0 us
    pallas_call x0 -> x1, Pallas kernels: none -> 8.43 us  [local(): pl.pallas_call(finish, out_shape=(jax.ShapeDtypeStruct((own, model), BF16...]
    unnamed x1 -> x0, local copies, waits for them, and re-layouts: 1.62 us -> none
    select_n x1 -> x0, other arithmetic: 1.37 us -> none  [local(): probe_values = jnp.where(live[None, :], values[:CH], jnp.zeros((), F32))]
where the time goes in v3:
time: 71.4 us; the launch traced here: 71.2 us
  Pallas kernels  69.9 us (98%)
  between operations  1.29 us (2%)
    pallas_call x1, Pallas kernels, local(): pl.pallas_call(functools.partial(body, (n_gx, n_gy, n_pa, rows, cols, mod...  61.5 us
    pallas_call x1, Pallas kernels, local(): pl.pallas_call(finish, out_shape=(jax.ShapeDtypeStruct((own, model), BF16...  8.43 us

profile of v3, /device:TPU:0, one launch (start us, length us, event | category | flops | bytes accessed | tf_op | source)
XLA Modules:
  0.0 71.2 jit_solution(7530593250160811093)
XLA Ops:
  1.3 61.5 %shard_map.167 = (bf16[128,768]{1,0:T(8,128)(2,1)}, f32[8,1024]{1,0:T(8,128)}) custom-call(bf16[128,768]{1,0:T(8,128)(2,1)} %bitcast.6, bf16[2,128,768]{2,1,0:T(8,128)(2,1)} %bitcast.5, f32[768]{0:T(1024)} %refs_2_.1, s32[1,1024]{1,0:T(1,128)} %bitcast.8, f32[2,1024]{1,0:T(2,128)} %refs_4_.1, bf16[384,128]{1,0:T(8,128)(2,1)} %constant.12.clone.refs_5_, ...), custom_call_target="tpu_custom_call" | custom-call | flops 6000000000 | bytes 4000000 | tf_op jit(solution)/shard_map/pallas_call | solution.py:509
  62.8 8.4 %shard_map.168 = (bf16[128,768]{1,0:T(8,128)(2,1)}, f32[3,1024]{1,0:T(4,128)}) custom-call(s32[1]{0:T(128)S(6)} %copy.18.count_ref, bf16[128,768]{1,0:T(8,128)(2,1)} %get-tuple-element.6.latent_ref, f32[8,1024]{1,0:T(8,128)} %get-tuple-element.7.value_ref), custom_call_target="tpu_custom_call" | custom-call | tf_op jit(solution)/shard_map/pallas_call | solution.py:520

commit v4 on v3

--- a/solution.py
+++ b/solution.py
@@ -441,12 +441,10 @@
         copy.wait_send()
 
 
-def finish(count_ref, latent_ref, value_ref, out_ref, val_ref, sem):
-    copy = pltpu.make_async_copy(latent_ref, out_ref, sem.at[0])
-    copy.start()
+def finish(count_ref, latent_ref, value_ref, out_ref, val_ref):
+    out_ref[...] = latent_ref[...]
     slot = lax.broadcasted_iota(jnp.int32, val_ref.shape, 1)
     val_ref[...] = jnp.where(slot < count_ref[0], value_ref[0:CH], 0.0)
-    copy.wait()
 
 
 def local(sizes, latents, noise, proc_gain, w_qkv, w_out, w_query, w_head, probe_cell, probe_offset, probe_count):
@@ -520,9 +518,8 @@
     latent_out, probe_values = pl.pallas_call(
         finish,
         out_shape=(jax.ShapeDtypeStruct((own, model), BF16), jax.ShapeDtypeStruct((CH, slots), F32)),
-        in_specs=[pl.BlockSpec(memory_space=pltpu.SMEM), apart, inside],
-        out_specs=[apart, inside],
-        scratch_shapes=[pltpu.SemaphoreType.DMA((1,))],
+        in_specs=[pl.BlockSpec(memory_space=pltpu.SMEM), inside, inside],
+        out_specs=[inside, inside],
         compiler_params=pltpu.CompilerParams(vmem_limit_bytes=VMEM_BYTES),
     )(probe_count, latent_out, values)
     return (latent_out.reshape(rows, cols, model), probe_values)

time: 71.4 us -> 64.6 us (0.905)
  Pallas kernels: 69.9 us -> 63.1 us
    pallas_call x1, Pallas kernels: 8.43 us -> 1.62 us  [local(): pl.pallas_call(finish, out_shape=(jax.ShapeDtypeStruct((own, model), BF16...]
where the time goes in v4:
time: 64.6 us; the launch traced here: 64.4 us
  Pallas kernels  63.1 us (98%)
  between operations  1.29 us (2%)
    pallas_call x1, Pallas kernels, local(): pl.pallas_call(functools.partial(body, (n_gx, n_gy, n_pa, rows, cols, mod...  61.5 us
    pallas_call x1, Pallas kernels, local(): pl.pallas_call(finish, out_shape=(jax.ShapeDtypeStruct((own, model), BF16...  1.62 us

profile of v4, /device:TPU:0, one launch (start us, length us, event | category | flops | bytes accessed | tf_op | source)
XLA Modules:
  0.0 64.4 jit_solution(15691085637275393246)
XLA Ops:
  1.3 61.5 %shard_map.167 = (bf16[128,768]{1,0:T(8,128)(2,1)}, f32[8,1024]{1,0:T(8,128)}) custom-call(bf16[128,768]{1,0:T(8,128)(2,1)} %bitcast.6, bf16[2,128,768]{2,1,0:T(8,128)(2,1)} %bitcast.5, f32[768]{0:T(1024)} %refs_2_.1, s32[1,1024]{1,0:T(1,128)} %bitcast.8, f32[2,1024]{1,0:T(2,128)} %refs_4_.1, bf16[384,128]{1,0:T(8,128)(2,1)} %constant.12.clone.refs_5_, ...), custom_call_target="tpu_custom_call" | custom-call | flops 6000000000 | bytes 4000000 | tf_op jit(solution)/shard_map/pallas_call | solution.py:507
  62.8 1.6 %shard_map.168 = (bf16[128,768]{1,0:T(8,128)(2,1)}, f32[3,1024]{1,0:T(4,128)}) custom-call(s32[1]{0:T(128)S(6)} %copy.18.count_ref, bf16[128,768]{1,0:T(8,128)(2,1)} %get-tuple-element.6.latent_ref, f32[8,1024]{1,0:T(8,128)} %get-tuple-element.7.value_ref), custom_call_target="tpu_custom_call" | custom-call | tf_op jit(solution)/shard_map/pallas_call | solution.py:518
